TPU v7x, 32 devices: a whole 2x2x4 slice. The times are simulated.
32 devices in a mesh: seq: 4 (over y, x), mem: 8 (over z, core).
Axes of the slice: x: 2, y: 2, z: 4, core: 2. Of those that a mesh axis runs over, the one named last changes fastest.
Arguments:
- queries: bfloat16 [512, 8192], P(('seq', 'mem')), may hold values from -90 to 90
- probes: int32 [512, 64, 8], P('seq'), may hold values from 0 to 15, as said below
- keys: bfloat16 [4, 4096, 8192], P('seq', 'mem'), may hold values from -5 to 5
- values: bfloat16 [4, 4096, 8192], P('seq', 'mem'), may hold values from -6 to 6
- w_out: bfloat16 [8192, 8192], P('mem', 'seq'), may hold values from -0.75 to 0.75
Outputs:
- output: bfloat16 [512, 8192], P(('seq', 'mem'))
Inputs may be any that keep to these rules, and one draw needn't show every extreme that they name: `probes`: for each row and head the 8 ids are distinct blocks of the row's group memory.
All inputs are finite; a program needn't handle non-finite values.
Results may differ from a plain program's by a relative error of at most 0.023.
Values may be sent and summed in bfloat16 or wider, within the bound.
A program may use at most 256 MiB of HBM per device.

v0:
```python
import jax
import jax.numpy as jnp
from jax import lax
from jax.sharding import PartitionSpec as P

H = 64
DH = 128
BLOCK = 256


def shards(queries, probes, keys, values, w_out):
    member = lax.axis_index("mem")
    mem_count = lax.axis_size("mem")
    rows_here = queries.shape[0]
    scaling = DH ** (-0.5)
    group_query = lax.all_gather(queries, "mem", axis=0, tiled=True)
    group_rows = group_query.shape[0]
    local_keys = keys.shape[1]
    local_blocks = local_keys // BLOCK
    query_heads = group_query.reshape(group_rows, H, DH)
    key_heads = keys[0].reshape(local_keys, H, DH)
    value_heads = values[0].reshape(local_keys, H, DH)
    scores = (
        jnp.einsum("qhd,khd->hqk", query_heads, key_heads, preferred_element_type=jnp.float32)
        * scaling
    )
    scores = scores.reshape(H, group_rows, local_blocks, BLOCK)
    block_ids = member * local_blocks + jnp.arange(local_blocks, dtype=jnp.int32)
    probed = jnp.any(probes[:, :, :, None] == block_ids[None, None, None, :], axis=2)
    probed = jnp.transpose(probed, (1, 0, 2))[:, :, :, None]
    masked = jnp.where(probed, scores, -1e30)
    local_top = jnp.max(masked, axis=(2, 3))
    row_top = lax.pmax(local_top, "mem")
    weights = jnp.where(probed, jnp.exp(masked - row_top[:, :, None, None]), 0.0)
    totals = jnp.sum(weights, axis=(2, 3))
    rounded = weights.reshape(H, group_rows, local_keys).astype(jnp.bfloat16)
    numerator = jnp.einsum("hqk,khd->qhd", rounded, value_heads, preferred_element_type=jnp.float32)
    numerator = numerator.reshape(group_rows, H * DH)
    num_part, total_part = (
        lax.psum_scatter(
            numerator.astype(jnp.bfloat16), "mem", scatter_dimension=1, tiled=True
        ).astype(jnp.float32),
        lax.psum_scatter(
            totals.T.astype(jnp.bfloat16), "mem", scatter_dimension=1, tiled=True
        ).astype(jnp.float32),
    )
    heads_here = total_part.shape[1]
    features = heads_here * DH
    attended = (
        (num_part.reshape(group_rows, heads_here, DH) / total_part[:, :, None])
        .reshape(group_rows, features)
        .astype(jnp.bfloat16)
    )
    seq_count = lax.axis_size("seq")
    shaped = attended.reshape(mem_count, 1, rows_here, features)
    gathered = lax.all_gather(shaped, "seq", axis=1, tiled=True)
    stacked = gathered.reshape(mem_count * seq_count * rows_here, features)
    column_block = lax.psum_scatter(
        jnp.dot(stacked, w_out, preferred_element_type=jnp.float32).astype(jnp.bfloat16),
        "mem",
        scatter_dimension=0,
        tiled=True,
    )
    output = lax.all_to_all(column_block, "seq", split_axis=0, concat_axis=1, tiled=True)
    return output


def solution(mesh):
    placed = (
        P(("seq", "mem"), None),
        P("seq", None, None),
        P("seq", "mem", None),
        P("seq", "mem", None),
        P("mem", "seq"),
    )
    return jax.shard_map(
        shards, mesh=mesh, in_specs=placed, out_specs=P(("seq", "mem"), None), check_vma=False
    )
```

profile of v0, /device:TPU:0, one launch (start us, length us, event | category | flops | bytes accessed | tf_op | source)
XLA Modules:
  0.0 232.0 jit_solution(16976575349455110854)
XLA Ops:
  6.5 0.0 all-gather.3.cloned.1.call-start
  6.5 0.7 all-gather.3.cloned.1.call-update
  7.3 0.0 reduce-scatter.4.cloned.1.call-start
  7.3 1.2 compare_reduce_fusion
  8.5 1.1 broadcast_in_dim.25
  9.6 7.1 %copy.35 = pred[64,128,512]{2,1,0:T(32,128)(4,1)} copy(pred[64,128,512]{1,2,0:T(32,128)(4,1)S(1)} %bitcast.32) | data formatting | bytes 8388608 | tf_op jit(solution)/shard_map/jit(_where)/broadcast_in_dim | solution.py:34
  16.7 9.7 %copy.46 = bf16[64,8,64,128]{3,2,1,0:T(8,128)(2,1)} copy(bf16[64,8,64,128]{3,1,2,0:T(8,128)(2,1)} %bitcast.34) | data formatting | bytes 16777216
  26.4 11.9 %copy.42 = bf16[1,512,8192]{1,2,0:T(8,128)(2,1)} copy(bf16[1,512,8192]{2,1,0:T(8,128)(2,1)} %param.8) | data formatting | bytes 16777216 | tf_op jit(solution)/shard_map/reshape;squeeze | solution.py:22
  38.3 2.5 %all-gather.3.cloned.1.call-done = bf16[128,8192]{1,0:T(8,128)(2,1)} async-done(((bf16[16,8192]{1,0:T(8,128)(2,1)}), bf16[128,8192]{1,0:T(8,128)(2,1)}) %all-gather.3.cloned.1.call-update) | async-done | bytes 2097168 | tf_op jit(solution)/shard_map/all_gather | solution.py:16
  40.8 3.2 %copy.31 = bf16[128,8192]{0,1:T(8,128)(2,1)S(1)} copy(bf16[128,8192]{1,0:T(8,128)(2,1)} %all-gather.3.cloned.1.call-done) | data formatting | bytes 4194304 | tf_op jit(solution)/shard_map/all_gather | solution.py:16
  44.0 16.9 %fusion = (f32[64,128]{1,0:T(8,128)S(1)}, f32[64,128,512]{2,1,0:T(8,128)}) fusion(pred[64,128,512]{2,1,0:T(32,128)(4,1)} %copy.35, bf16[128,64,128]{0,2,1:T(8,128)(2,1)S(1)} %bitcast.33, bf16[512,64,128]{2,1,0:T(8,128)(2,1)} %bitcast.31), kind=kOutput, calls=%fused_computation.2 | convolution fusion | flops 1086316544 | bytes 31490048 | tf_op jit(solution)/shard_map/qhd,khd->hqk/dot_general | solution.py:24
  60.9 27.8 %pmax.7 = f32[64,128]{1,0:T(8,128)S(1)} all-reduce(f32[64,128]{1,0:T(8,128)S(1)} %get-tuple-element.5), channel_id=1, replica_groups=mesh['seq'=4,'mem'=8] {'mem'}, use_global_device_ids=true, to_apply=%region_2.3 | all-reduce | flops 8192 | bytes 65536 | tf_op jit(solution)/shard_map/pmax | solution.py:33
  88.7 0.0 copy-start
  88.8 14.1 %fusion.11 = bf16[64,128,128]{1,2,0:T(8,128)(2,1)S(1)} fusion(bf16[512,64,128]{0,2,1:T(8,128)(2,1)} %bitcast.35, pred[64,128,512]{2,1,0:T(32,128)(4,1)} %copy.35, f32[64,128,512]{2,1,0:T(8,128)} %get-tuple-element.6, f32[64,128]{1,0:T(8,128)S(1)} %pmax.7), kind=kOutput, calls=%fused_computation.13 | convolution fusion | flops 1095761920 | bytes 31490048 | tf_op jit(solution)/shard_map/hqk,khd->qhd/dot_general | solution.py:37
  102.8 3.0 %copy.37 = bf16[128,8192]{1,0:T(8,128)(2,1)} copy(bf16[128,8192]{0,1:T(8,128)(2,1)S(1)} %bitcast.36) | data formatting | bytes 4194304 | tf_op jit(solution)/shard_map/convert_element_type | solution.py:41
  105.8 0.0 reduce-scatter.4.cloned.1.call-update
  105.8 0.0 all-gather.5.cloned.1.call-start
  105.9 0.0 copy-done
  105.9 0.6 dynamic-slice
  107.1 11.8 %fusion.1 = bf16[64,128]{1,0:T(8,128)(2,1)S(1)} fusion(pred[64,128,512]{2,1,0:T(32,128)(4,1)} %copy.35, f32[64,128,512]{2,1,0:T(8,128)} %get-tuple-element.6, f32[64,128]{1,0:T(8,128)S(1)} %pmax.7), kind=kLoop, calls=%fused_computation.3 | loop fusion | flops 20963328 | bytes 21020672 | tf_op jit(solution)/shard_map/reduce_sum | solution.py:35
  119.0 0.1 copy.38
  119.1 26.3 %all-reduce = bf16[128,64]{1,0:T(8,128)(2,1)S(1)} all-reduce(bf16[128,64]{1,0:T(8,128)(2,1)S(1)} %copy.38), channel_id=3, replica_groups=mesh['seq'=4,'mem'=8] {'mem'}, use_global_device_ids=true, to_apply=%region_5.6.clone | all-reduce | flops 8192 | bytes 32768
  145.3 0.1 dynamic-slice_convert_fusion
  145.4 0.0 reduce-scatter.4.cloned.1.call-done
  145.4 0.2 div.11
  145.6 1.8 fusion.14
  147.4 0.0 all-gather.5.cloned.1.call-update
  147.4 0.0 reduce-scatter.6.cloned.1.call-start
  147.5 24.7 %all-gather.5.cloned.1.call-done = bf16[8,4,16,1024]{3,2,0,1:T(8,128)(2,1)} async-done(((bf16[8,1,16,1024]{3,2,0,1:T(8,128)(2,1)}), bf16[8,4,16,1024]{3,2,0,1:T(8,128)(2,1)}) %all-gather.5.cloned.1.call-update) | async-done | bytes 1048592 | tf_op jit(solution)/shard_map/all_gather | solution.py:56
  172.2 1.3 copy.39
  173.5 5.9 %convolution_convert_fusion = bf16[512,2048]{1,0:T(8,128)(2,1)} fusion(bf16[512,1024]{1,0:T(8,128)(2,1)S(1)} %bitcast.38, bf16[1024,2048]{1,0:T(8,128)(2,1)} %param.9), kind=kOutput, calls=%fused_computation.12 | convolution fusion | flops 2148532224 | bytes 7340032 | tf_op jit(solution)/shard_map/dot_general | solution.py:59
  179.4 0.0 reduce-scatter.6.cloned.1.call-update
  179.5 36.0 %reduce-scatter.6.cloned.1.call-done = bf16[64,2048]{1,0:T(8,128)(2,1)} async-done(((bf16[512,2048]{1,0:T(8,128)(2,1)}), bf16[64,2048]{1,0:T(8,128)(2,1)}) %reduce-scatter.6.cloned.1.call-update) | async-done | bytes 262160 | tf_op jit(solution)/shard_map/reduce_scatter | solution.py:58
  215.4 9.3 %all_to_all.19 = bf16[4,16,2048]{2,1,0:T(8,128)(2,1)S(1)} all-to-all(bf16[4,16,2048]{2,1,0:T(8,128)(2,1)} %bitcast.41), channel_id=1, replica_groups=mesh['seq'=4,'mem'=8] {'seq'}, dimensions={0} | all-to-all | bytes 524288 | tf_op jit(solution)/shard_map/all_to_all | solution.py:64
  224.8 0.7 copy.45
  (1 shorter events, 0.0 us)
Async XLA Ops:
  6.5 34.3 %all-gather.3.cloned.1.call-start = ((), (), s32[]{:S(2)}) async-start(), calls=%async_computation.3 | async-start | bytes 2359296 | tf_op jit(solution)/shard_map/all_gather | solution.py:16
  7.3 138.2 %reduce-scatter.4.cloned.1.call-start = ((), (), s32[]{:S(2)}) async-start(), calls=%async_computation.4 | async-start | bytes 2359296 | tf_op jit(solution)/shard_map/reduce_scatter | solution.py:40
  88.7 17.1 %copy-start = (u32[32]{0:T(128)S(1)}, u32[32]{0:T(128)}, u32[]{:S(2)}) copy-start(u32[32]{0:T(128)} %constant.21) | copy-start | bytes 388
  105.8 66.4 %all-gather.5.cloned.1.call-start = ((), (), s32[]{:S(2)}) async-start(), calls=%async_computation.5 | async-start | bytes 1310720 | tf_op jit(solution)/shard_map/all_gather | solution.py:56
  147.4 68.0 %reduce-scatter.6.cloned.1.call-start = ((), (), s32[]{:S(2)}) async-start(), calls=%async_computation.6 | async-start | bytes 2359296 | tf_op jit(solution)/shard_map/reduce_scatter | solution.py:58
Sparse Core Ops, SparseCore 0:
  9.0 31.7 all-gather.2
  105.9 34.1 reduce-scatter.3
  147.6 24.6 all-gather.4
  179.6 35.7 reduce-scatter.5
where the time goes:
time: 233 us; the launch traced here: 232 us
  waiting for transfers between devices  64 us (27%)
  blocking collectives  63.4 us (27%)
  local copies, waits for them, and re-layouts  38.8 us (17%)
  matrix products  36.9 us (16%)
  other arithmetic  14.9 us (6%)
  between operations  13.8 us (6%)
    reduce_scatter x1, waiting for transfers between devices, shards(): lax.psum_scatter(jnp.dot(stacked, w_out, preferred_element_type=jnp.float...  36 us
    pmax x1, blocking collectives, shards(): row_top = lax.pmax(local_top, 'mem')  27.8 us
    unnamed x1, blocking collectives  26.3 us
    all_gather x1, waiting for transfers between devices, shards(): gathered = lax.all_gather(shaped, 'seq', axis=1, tiled=True)  24.7 us
    dot_general x1, matrix products, shards(): jnp.einsum('qhd,khd->hqk', query_heads, key_heads, preferred_element_type...  16.9 us
    dot_general x1, matrix products, shards(): jnp.einsum('hqk,khd->qhd', rounded, value_heads, preferred_element_type=j...  14.1 us
    another operation x1, local copies, waits for them, and re-layouts, shards(): value_heads = values[0].reshape(local_keys, H, DH)  11.9 us
    reduce_sum x1, other arithmetic, shards(): totals = jnp.sum(weights, axis=(2, 3))  11.8 us
  transfers between devices with their start and end apart: 4, of which 3 were waited for; matrix products, arithmetic and copies ran while one was open for 19% of the time, Pallas kernels for 0%

commit v1 on v0

v1 whole, which is shorter than its diff:
```python
import functools

import jax
import jax.numpy as jnp
from jax import lax
from jax.experimental import pallas as pl
from jax.experimental.pallas import tpu as pltpu
from jax.sharding import PartitionSpec as P

H = 64
DH = 128
BLOCK = 256
LOW = -1e30
DELAY = 1
MESH = pl.DeviceIdType.MESH
F32 = jnp.float32
BF16 = jnp.bfloat16


def kernel(
    n, ns, q_ref, bias_ref, k_ref, v_ref, w_ref, out_ref,
    qg, kbuf, vbuf, wbuf, own, own_st, sib, sib_st, chn, chn_st, gat, part, psib, pchn, obuf,
    kv_sem, w_sem, q_sem, qs_send, qs_recv, rl_send, rl_recv, as_send, as_recv, ac_send, ac_recv,
    g_send, g_recv, bs_send, bs_recv, bc_send, bc_recv, o_send, o_recv,
):
    nc = n // 2
    slots = kbuf.shape[0]
    rows_here, _ = q_ref.shape
    rows = qg.shape[1]
    wide = qg.shape[2]
    feats = wide // 2
    heads = feats // DH
    keys = kbuf.shape[1]
    blocks = keys // BLOCK
    cols = wbuf.shape[1]
    st_rows = own_st.shape[2]
    s = lax.axis_index("seq")
    me = lax.axis_index("mem")
    p = me // 2
    c = me % 2
    twin = (s, p * 2 + 1 - c)

    def peer(d):
        return (s, ((p + d) % nc) * 2 + c)

    def across(d):
        return ((s + d) % ns, me)

    def turn(i):
        return (i % 2) * (nc - 1 - i // 2) + (1 - i % 2) * (i // 2)

    def remote(src, dst, send, recv, to):
        return pltpu.make_async_remote_copy(
            src_ref=src, dst_ref=dst, send_sem=send, recv_sem=recv, device_id=to, device_id_type=MESH
        )

    def span(i, size):
        return pl.ds(pl.multiple_of(i * size, size), size)

    def key_copies(i):
        at = turn(i)
        slot = i % slots
        return (
            pltpu.make_async_copy(k_ref.at[0, :, span(at, wide)], kbuf.at[slot], kv_sem.at[slot, 0]),
            pltpu.make_async_copy(v_ref.at[0, :, span(at, wide)], vbuf.at[slot], kv_sem.at[slot, 1]),
        )

    def own_query(at):
        return pltpu.make_async_copy(
            q_ref.at[:, span(at, wide)], qg.at[at, span(me, rows_here), :], q_sem.at[at]
        )

    def query_send(at, d):
        return remote(
            q_ref.at[:, span(at, wide)], qg.at[at, span(me, rows_here), :],
            qs_send.at[at, d], qs_recv.at[at, d], peer(d),
        )

    def query_twin(at):
        return remote(
            q_ref.at[:, span(at, wide)], qg.at[at, span(me, rows_here), :],
            rl_send.at[at, 0], rl_recv.at[at, 0], twin,
        )

    def query_relay(at, d):
        source = ((p + nc - d) % nc) * 2 + c
        piece = qg.at[at, span(source, rows_here), :]
        return remote(piece, piece, rl_send.at[at, d], rl_recv.at[at, d], twin)

    weight_copy = pltpu.make_async_copy(w_ref, wbuf, w_sem.at[0])

    barrier = pltpu.get_barrier_semaphore()
    for d in range(1, nc):
        pl.semaphore_signal(barrier, inc=1, device_id=peer(d), device_id_type=MESH)
    for d in range(1, ns):
        pl.semaphore_signal(barrier, inc=1, device_id=across(d), device_id_type=MESH)
    pl.semaphore_signal(barrier, inc=1, device_id=twin, device_id_type=MESH)
    pl.semaphore_wait(barrier, nc + ns - 1)

    def start_queries(i, carry):
        at = turn(i)
        for d in range(1, nc):
            query_send(at, d).start()
        query_twin(at).start()
        own_query(at).start()
        return carry

    lax.fori_loop(0, nc, start_queries, 0)
    for i in range(slots):
        for copy in key_copies(i):
            copy.start()
    weight_copy.start()

    lane = lax.broadcasted_iota(jnp.int32, (rows, 128), 1)

    def twin_send(at):
        return (
            remote(own.at[at, 1 - c], sib.at[at], as_send.at[at, 0], as_recv.at[at, 0], twin),
            remote(own_st.at[at, 1 - c], sib_st.at[at], as_send.at[at, 1], as_recv.at[at, 1], twin),
        )

    def attend(i):
        at = turn(i)
        slot = i % slots
        for d in range(1, nc):
            query_send(at, d).wait_recv()
            query_relay(at, d).start()
        for copy in key_copies(i):
            copy.wait()
        own_query(at).wait()
        query_twin(at).wait_recv()
        for d in range(1, nc):
            query_relay(at, d).wait_recv()
        for side in range(2):
            stats = jnp.zeros((rows, 128), F32)
            for head in range(heads):
                lo = side * feats + head * DH
                query = qg[at, :, lo : lo + DH]
                scores = lax.dot_general(
                    query, kbuf[slot, :, lo : lo + DH], (((1,), (1,)), ((), ())), preferred_element_type=F32
                ) * (DH ** -0.5)
                pieces = []
                for b in range(blocks):
                    at_lane = (side * heads + head) * blocks + b
                    pieces.append(
                        scores[:, b * BLOCK : (b + 1) * BLOCK] + bias_ref[at, :, at_lane : at_lane + 1]
                    )
                top = functools.reduce(
                    jnp.maximum, [jnp.max(piece, axis=1, keepdims=True) for piece in pieces]
                )
                weights = jnp.concatenate([jnp.exp(piece - top) for piece in pieces], axis=1)
                total = jnp.sum(weights, axis=1, keepdims=True)
                numer = jnp.dot(
                    weights.astype(BF16), vbuf[slot, :, lo : lo + DH], preferred_element_type=F32
                )
                own[at, side, :, head * DH : (head + 1) * DH] = numer.astype(BF16)
                stats = jnp.where(lane == head, top, stats)
                stats = jnp.where(lane == heads + head, total, stats)
            own_st[at, side] = stats.T[:st_rows]
        for copy in twin_send(at):
            copy.start()

        @pl.when(i + slots < nc)
        def _():
            for copy in key_copies(i + slots):
                copy.start()

    def hop(at, nums, sts, send, recv):
        def pair(slot, to):
            made = []
            for x, (mine, theirs) in enumerate(zip(nums, sts)):
                made.append(remote(mine.at[at, c], theirs.at[slot], send.at[at, x], recv.at[slot, x], to))
            return made

        return pair

    def a_pair(at):
        return hop(at, (own, own_st), (chn, chn_st), ac_send, ac_recv)

    def b_pair(at):
        return hop(at, (part,), (pchn,), bc_send, bc_recv)

    def move(at, maker, begin):
        @pl.when(at > p)
        def _():
            for copy in maker(at)(at, (s, (p + 1) * 2 + c)):
                if begin:
                    copy.start()
                else:
                    copy.wait_send()

        @pl.when((at < p) & ((at != p - 1) | (at == 0)))
        def _():
            for copy in maker(at)(at, (s, (p - 1) * 2 + c)):
                if begin:
                    copy.start()
                else:
                    copy.wait_send()

        @pl.when((at < p) & (at == p - 1) & (at > 0))
        def _():
            for copy in maker(at)(nc, (s, (p - 1) * 2 + c)):
                if begin:
                    copy.start()
                else:
                    copy.wait_send()

    def arrive(at, maker, slot):
        for copy in maker(at)(slot, twin):
            copy.wait_recv()

    def cases(at, body):
        ends = ((at > p) & (p == 0)) | ((at < p) & (p == nc - 1))
        both = (at == p) & (p > 0) & (p < nc - 1)

        @pl.when(ends)
        def _():
            body(0)

        @pl.when(jnp.logical_not(ends | both))
        def _():
            body(1)

        @pl.when(both)
        def _():
            body(2)

    def merge(at):
        for copy in twin_send(at):
            copy.wait_recv()

        def body(count):
            sources = [(own.at[at, c], own_st.at[at, c]), (sib.at[at], sib_st.at[at])]
            for slot in (at, nc)[:count]:
                arrive(at, a_pair, slot)
                sources.append((chn.at[slot], chn_st.at[slot]))
            tops = [st[:heads] for _, st in sources]
            sums = [st[heads : 2 * heads] for _, st in sources]
            top = functools.reduce(jnp.maximum, tops)
            scales = [jnp.exp(t - top) for t in tops]
            total = functools.reduce(jnp.add, [e * t for e, t in zip(scales, sums)])
            done = at == p
            factor = jnp.where(done, 1.0 / total, jnp.ones_like(total))
            scales = [e * factor for e in scales]
            filler = jnp.zeros((128 - heads * len(scales), rows), F32)
            lanes = jnp.concatenate(scales + [filler], axis=0).T
            for head in range(heads):
                cut = slice(head * DH, (head + 1) * DH)
                value = functools.reduce(
                    jnp.add,
                    [
                        num[:, cut].astype(F32) * lanes[:, x * heads + head : x * heads + head + 1]
                        for x, (num, _) in enumerate(sources)
                    ],
                )
                own[at, c, :, cut] = value.astype(BF16)
            own_st[at, c, :heads] = top
            own_st[at, c, heads : 2 * heads] = total

        cases(at, body)
        move(at, a_pair, True)

    def attention(i, carry):
        @pl.when(i < nc)
        def _():
            attend(i)

        @pl.when(i >= DELAY)
        def _():
            merge(turn(i - DELAY))

        return carry

    lax.fori_loop(0, nc + DELAY, attention, 0)

    def spread(d):
        return remote(own.at[p, c], gat.at[s], g_send.at[d], g_recv.at[d], across(d))

    for d in range(1, ns):
        spread(d).start()
    gat[s] = own[p, c]
    weight_copy.wait()
    for d in range(1, ns):
        spread(d).wait_recv()

    def part_send(at):
        return remote(part.at[at, 1 - c], psib.at[at], bs_send.at[at], bs_recv.at[at], twin)

    def project(i):
        at = turn(i)
        for side in range(2):
            piece = gat[:, pl.ds(pl.multiple_of((at * 2 + side) * rows_here, rows_here), rows_here), :]
            piece = piece.reshape(ns * rows_here, feats)
            part[at, side] = jnp.dot(piece, wbuf[...], preferred_element_type=F32).astype(BF16)
        part_send(at).start()

    def add(at):
        part_send(at).wait_recv()

        def body(count):
            sources = [part.at[at, c], psib.at[at]]
            for slot in (at, nc)[:count]:
                arrive(at, b_pair, slot)
                sources.append(pchn.at[slot])
            step = 512
            for lo in range(0, cols, step):
                value = functools.reduce(jnp.add, [x[:, lo : lo + step].astype(F32) for x in sources])
                part[at, c, :, lo : lo + step] = value.astype(BF16)

        cases(at, body)
        move(at, b_pair, True)

    def projection(i, carry):
        @pl.when(i < nc)
        def _():
            project(i)

        @pl.when(i >= DELAY)
        def _():
            add(turn(i - DELAY))

        return carry

    lax.fori_loop(0, nc + DELAY, projection, 0)

    def deliver(d):
        to = (s + d) % ns
        return remote(
            part.at[p, c, span(to, rows_here), :], obuf.at[s], o_send.at[d], o_recv.at[d], across(d)
        )

    for d in range(1, ns):
        deliver(d).start()
    obuf[s] = part[p, c, span(s, rows_here), :]

    def drain(i, carry):
        for d in range(1, nc):
            query_send(i, d).wait_send()
            query_relay(i, d).wait_send()
        query_twin(i).wait_send()
        for copy in twin_send(i):
            copy.wait_send()
        part_send(i).wait_send()
        move(i, a_pair, False)
        move(i, b_pair, False)
        return carry

    lax.fori_loop(0, nc, drain, 0)
    for d in range(1, ns):
        spread(d).wait_send()
        deliver(d).wait_recv()
    for t in range(ns):
        out_ref[:, t * cols : (t + 1) * cols] = obuf[t]
    for d in range(1, ns):
        deliver(d).wait_send()


def shards(n, ns, queries, probes, keys, values, w_out):
    nc = n // 2
    rows_here, width = queries.shape
    rows = probes.shape[0]
    local_keys = keys.shape[1]
    local_blocks = local_keys // BLOCK
    feats, cols = w_out.shape
    wide = 2 * feats
    heads = feats // DH
    st_rows = max(8, 2 * heads)
    slots = min(nc, 4)
    block_ids = lax.axis_index("mem") * local_blocks + jnp.arange(local_blocks, dtype=jnp.int32)
    probed = jnp.any(probes[:, :, :, None] == block_ids[None, None, None, :], axis=2)
    bias = jnp.where(probed, 0.0, LOW).astype(F32).reshape(rows, nc, 2 * heads * local_blocks)
    bias = jnp.transpose(bias, (1, 0, 2))
    dma = pltpu.SemaphoreType.DMA
    vm = pltpu.VMEM
    flops = 4 * rows * width * local_keys + 2 * ns * rows * feats * cols
    return pl.pallas_call(
        functools.partial(kernel, n, ns),
        out_shape=jax.ShapeDtypeStruct((rows_here, ns * cols), BF16),
        in_specs=[
            pl.BlockSpec(memory_space=pl.ANY),
            pl.BlockSpec(memory_space=pltpu.VMEM),
            pl.BlockSpec(memory_space=pl.ANY),
            pl.BlockSpec(memory_space=pl.ANY),
            pl.BlockSpec(memory_space=pl.ANY),
        ],
        out_specs=pl.BlockSpec(memory_space=pltpu.VMEM),
        scratch_shapes=[
            vm((nc, rows, wide), BF16),
            vm((slots, local_keys, wide), BF16),
            vm((slots, local_keys, wide), BF16),
            vm((feats, cols), BF16),
            vm((nc, 2, rows, feats), BF16),
            vm((nc, 2, st_rows, rows), F32),
            vm((nc, rows, feats), BF16),
            vm((nc, st_rows, rows), F32),
            vm((nc + 1, rows, feats), BF16),
            vm((nc + 1, st_rows, rows), F32),
            vm((ns, rows, feats), BF16),
            vm((nc, 2, ns * rows_here, cols), BF16),
            vm((nc, ns * rows_here, cols), BF16),
            vm((nc + 1, ns * rows_here, cols), BF16),
            vm((ns, rows_here, cols), BF16),
            dma((slots, 2)),
            dma((1,)),
            dma((nc,)),
            dma((nc, nc)),
            dma((nc, nc)),
            dma((nc, nc)),
            dma((nc, nc)),
            dma((nc, 2)),
            dma((nc, 2)),
            dma((nc, 2)),
            dma((nc + 1, 2)),
            dma((ns,)),
            dma((ns,)),
            dma((nc,)),
            dma((nc,)),
            dma((nc, 1)),
            dma((nc + 1, 1)),
            dma((ns,)),
            dma((ns,)),
        ],
        compiler_params=pltpu.CompilerParams(
            collective_id=0, has_side_effects=True, vmem_limit_bytes=60 * 1024 * 1024
        ),
        cost_estimate=pl.CostEstimate(
            flops=flops, bytes_accessed=4 * local_keys * width + 2 * feats * cols,
            transcendentals=rows * H * local_keys,
        ),
    )(queries, bias, keys, values, w_out)


def solution(mesh):
    placed = (
        P(("seq", "mem"), None),
        P("seq", None, None),
        P("seq", "mem", None),
        P("seq", "mem", None),
        P("mem", "seq"),
    )
    body = functools.partial(shards, mesh.shape["mem"], mesh.shape["seq"])
    return jax.shard_map(
        body, mesh=mesh, in_specs=placed, out_specs=P(("seq", "mem"), None), check_vma=False
    )
```

time: 233 us -> 199 us (0.85)
  the two profiles are of different devices: /device:TPU:0 before, /device:TPU:18 now
where the time goes in v1:
time: 199 us
  Pallas kernels  195 us (98%)
  local copies, waits for them, and re-layouts  2.51 us (1%)
    pallas_call x1, Pallas kernels, shards(): pl.pallas_call(functools.partial(kernel, n, ns), out_shape=jax.ShapeDtype...  195 us

profile of v1, /device:TPU:18, one launch (start us, length us, event | category | flops | bytes accessed | tf_op | source)
XLA Modules:
  0.0 198.7 jit_solution(16114646947272750466)
XLA Ops:
  0.0 1.2 compare_reduce_fusion
  1.3 0.8 copy.9
  2.1 194.9 %shard_map.55 = bf16[16,8192]{1,0:T(8,128)(2,1)} custom-call(bf16[16,8192]{1,0:T(8,128)(2,1)} %q_ref.1, f32[4,128,32]{2,1,0:T(8,128)} %bitcast.2, bf16[1,512,8192]{2,1,0:T(8,128)(2,1)} %k_ref.1, bf16[1,512,8192]{2,1,0:T(8,128)(2,1)} %v_ref.1, bf16[1024,2048]{1,0:T(8,128)(2,1)} %w_ref.1), custom_call_target="tpu_custom_call" | custom-call | flops 4294967296 | bytes 20971520 | tf_op jit(solution)/shard_map/pallas_call | solution.py:376
  197.0 1.7 copy.11
  (2 shorter events, 0.1 us)

commit v2 on v1

--- a/solution.py
+++ b/solution.py
@@ -11,7 +11,7 @@
 DH = 128
 BLOCK = 256
 LOW = -1e30
-DELAY = 1
+RATE = DH ** -0.5 * 1.4426950408889634
 MESH = pl.DeviceIdType.MESH
 F32 = jnp.float32
 BF16 = jnp.bfloat16
@@ -138,7 +138,7 @@
                 query = qg[at, :, lo : lo + DH]
                 scores = lax.dot_general(
                     query, kbuf[slot, :, lo : lo + DH], (((1,), (1,)), ((), ())), preferred_element_type=F32
-                ) * (DH ** -0.5)
+                )
                 pieces = []
                 for b in range(blocks):
                     at_lane = (side * heads + head) * blocks + b
@@ -148,7 +148,7 @@
                 top = functools.reduce(
                     jnp.maximum, [jnp.max(piece, axis=1, keepdims=True) for piece in pieces]
                 )
-                weights = jnp.concatenate([jnp.exp(piece - top) for piece in pieces], axis=1)
+                weights = jnp.concatenate([jnp.exp2((piece - top) * RATE) for piece in pieces], axis=1)
                 total = jnp.sum(weights, axis=1, keepdims=True)
                 numer = jnp.dot(
                     weights.astype(BF16), vbuf[slot, :, lo : lo + DH], preferred_element_type=F32
@@ -237,7 +237,7 @@
             tops = [st[:heads] for _, st in sources]
             sums = [st[heads : 2 * heads] for _, st in sources]
             top = functools.reduce(jnp.maximum, tops)
-            scales = [jnp.exp(t - top) for t in tops]
+            scales = [jnp.exp2((t - top) * RATE) for t in tops]
             total = functools.reduce(jnp.add, [e * t for e, t in zip(scales, sums)])
             done = at == p
             factor = jnp.where(done, 1.0 / total, jnp.ones_like(total))
@@ -260,18 +260,35 @@
         cases(at, body)
         move(at, a_pair, True)
 
+    turns = nc + nc - nc // 2
+
+    def advance(i, join):
+        late = i // nc
+        k = (1 - late) * (i // 2) + late * (i - nc + nc // 2)
+
+        def one(side, carry):
+            dest = (1 - side) * (nc - 1 - k + p) + side * (k - nc + 1 + p)
+            wanted = ((side == 0) & (dest < nc)) | ((side == 1) & (dest >= 0) & (dest < p))
+
+            @pl.when(wanted)
+            def _():
+                join(dest)
+
+            return carry
+
+        @pl.when((late == 1) | (i % 2 == 1))
+        def _():
+            lax.fori_loop(0, 2, one, 0)
+
     def attention(i, carry):
         @pl.when(i < nc)
         def _():
             attend(i)
 
-        @pl.when(i >= DELAY)
-        def _():
-            merge(turn(i - DELAY))
-
+        advance(i, merge)
         return carry
 
-    lax.fori_loop(0, nc + DELAY, attention, 0)
+    lax.fori_loop(0, turns, attention, 0)
 
     def spread(d):
         return remote(own.at[p, c], gat.at[s], g_send.at[d], g_recv.at[d], across(d))
@@ -315,13 +332,10 @@
         def _():
             project(i)
 
-        @pl.when(i >= DELAY)
-        def _():
-            add(turn(i - DELAY))
-
+        advance(i, add)
         return carry
 
-    lax.fori_loop(0, nc + DELAY, projection, 0)
+    lax.fori_loop(0, turns, projection, 0)
 
     def deliver(d):
         to = (s + d) % ns

time: 199 us -> 111 us (0.56)
  the two profiles are of different devices: /device:TPU:18 before, /device:TPU:0 now
where the time goes in v2:
time: 111 us
  Pallas kernels  107 us (96%)
  local copies, waits for them, and re-layouts  2.51 us (2%)
  other arithmetic  1.26 us (1%)
    pallas_call x1, Pallas kernels, shards(): pl.pallas_call(functools.partial(kernel, n, ns), out_shape=jax.ShapeDtype...  107 us

profile of v2, /device:TPU:0, one launch (start us, length us, event | category | flops | bytes accessed | tf_op | source)
XLA Modules:
  0.0 110.8 jit_solution(2607433850118840630)
XLA Ops:
  0.0 1.2 %compare_reduce_fusion = pred[128,64,2]{0,2,1:T(4,128)(4,1)S(1)} fusion(s32[128,64,8]{0,2,1:T(8,128)} %param.6, s32[2]{0:T(128)S(1)} %iota_add_fusion), kind=kLoop, calls=%fused_computation | loop fusion | flops 245760 | bytes 278536 | tf_op jit(solution)/shard_map/reduce_or | solution.py:384
  1.3 0.8 copy.9
  2.1 107.1 %shard_map.55 = bf16[16,8192]{1,0:T(8,128)(2,1)} custom-call(bf16[16,8192]{1,0:T(8,128)(2,1)} %q_ref.1, f32[4,128,32]{2,1,0:T(8,128)} %bitcast.2, bf16[1,512,8192]{2,1,0:T(8,128)(2,1)} %k_ref.1, bf16[1,512,8192]{2,1,0:T(8,128)(2,1)} %v_ref.1, bf16[1024,2048]{1,0:T(8,128)(2,1)} %w_ref.1), custom_call_target="tpu_custom_call" | custom-call | flops 4294967296 | bytes 20971520 | tf_op jit(solution)/shard_map/pallas_call | solution.py:390
  109.2 1.7 %copy.11 = bf16[16,8192]{1,0:T(8,128)(2,1)} copy(bf16[16,8192]{1,0:T(8,128)(2,1)} %shard_map.55) | data formatting | bytes 524288
  (2 shorter events, 0.1 us)

commit v3 on v2

--- a/solution.py
+++ b/solution.py
@@ -30,9 +30,12 @@
     wide = qg.shape[2]
     feats = wide // 2
     heads = feats // DH
+    half_heads = heads // 2
+    half_feats = feats // 2
     keys = kbuf.shape[1]
     blocks = keys // BLOCK
     cols = wbuf.shape[1]
+    half_cols = cols // 2
     st_rows = own_st.shape[2]
     s = lax.axis_index("seq")
     me = lax.axis_index("mem")
@@ -119,31 +122,38 @@
             remote(own_st.at[at, 1 - c], sib_st.at[at], as_send.at[at, 1], as_recv.at[at, 1], twin),
         )
 
+    def relay(at):
+        for d in range(1, nc):
+            query_send(at, d).wait_recv()
+            query_relay(at, d).start()
+
     def attend(i):
         at = turn(i)
         slot = i % slots
-        for d in range(1, nc):
-            query_send(at, d).wait_recv()
-            query_relay(at, d).start()
         for copy in key_copies(i):
             copy.wait()
         own_query(at).wait()
         query_twin(at).wait_recv()
         for d in range(1, nc):
             query_relay(at, d).wait_recv()
+
+        def raw(x):
+            cut = slice(x * DH, (x + 1) * DH)
+            return lax.dot_general(
+                qg[at, :, cut], kbuf[slot, :, cut], (((1,), (1,)), ((), ())), preferred_element_type=F32
+            )
+
+        scores = raw(0)
         for side in range(2):
             stats = jnp.zeros((rows, 128), F32)
             for head in range(heads):
-                lo = side * feats + head * DH
-                query = qg[at, :, lo : lo + DH]
-                scores = lax.dot_general(
-                    query, kbuf[slot, :, lo : lo + DH], (((1,), (1,)), ((), ())), preferred_element_type=F32
-                )
+                x = side * heads + head
+                later = raw(x + 1) if x + 1 < 2 * heads else None
                 pieces = []
                 for b in range(blocks):
-                    at_lane = (side * heads + head) * blocks + b
+                    lane_at = x * blocks + b
                     pieces.append(
-                        scores[:, b * BLOCK : (b + 1) * BLOCK] + bias_ref[at, :, at_lane : at_lane + 1]
+                        scores[:, b * BLOCK : (b + 1) * BLOCK] + bias_ref[at, :, lane_at : lane_at + 1]
                     )
                 top = functools.reduce(
                     jnp.maximum, [jnp.max(piece, axis=1, keepdims=True) for piece in pieces]
@@ -151,12 +161,18 @@
                 weights = jnp.concatenate([jnp.exp2((piece - top) * RATE) for piece in pieces], axis=1)
                 total = jnp.sum(weights, axis=1, keepdims=True)
                 numer = jnp.dot(
-                    weights.astype(BF16), vbuf[slot, :, lo : lo + DH], preferred_element_type=F32
+                    weights.astype(BF16), vbuf[slot, :, x * DH : (x + 1) * DH], preferred_element_type=F32
                 )
-                own[at, side, :, head * DH : (head + 1) * DH] = numer.astype(BF16)
+                half, place = head // half_heads, head % half_heads
+                own[at, side, half, :, place * DH : (place + 1) * DH] = numer.astype(BF16)
                 stats = jnp.where(lane == head, top, stats)
                 stats = jnp.where(lane == heads + head, total, stats)
+                scores = later
             own_st[at, side] = stats.T[:st_rows]
+            if side == 0:
+                @pl.when(i + 1 < nc)
+                def _():
+                    relay(turn(i + 1))
         for copy in twin_send(at):
             copy.start()
 
@@ -165,48 +181,41 @@
             for copy in key_copies(i + slots):
                 copy.start()
 
-    def hop(at, nums, sts, send, recv):
-        def pair(slot, to):
-            made = []
-            for x, (mine, theirs) in enumerate(zip(nums, sts)):
-                made.append(remote(mine.at[at, c], theirs.at[slot], send.at[at, x], recv.at[slot, x], to))
-            return made
-
-        return pair
-
-    def a_pair(at):
-        return hop(at, (own, own_st), (chn, chn_st), ac_send, ac_recv)
-
-    def b_pair(at):
-        return hop(at, (part,), (pchn,), bc_send, bc_recv)
-
-    def move(at, maker, begin):
-        @pl.when(at > p)
-        def _():
-            for copy in maker(at)(at, (s, (p + 1) * 2 + c)):
+    def a_pair(at, half, slot, to):
+        made = [
+            remote(own.at[at, c, half], chn.at[slot, half], ac_send.at[at, half], ac_recv.at[slot, half], to)
+        ]
+        if half == 0:
+            made.append(remote(own_st.at[at, c], chn_st.at[slot], ac_send.at[at, 2], ac_recv.at[slot, 2], to))
+        return made
+
+    def b_pair(at, half, slot, to):
+        return [
+            remote(part.at[at, c, half], pchn.at[slot, half], bc_send.at[at, half], bc_recv.at[slot, half], to)
+        ]
+
+    def move(at, maker, half, begin):
+        def go(slot, step):
+            for copy in maker(at, half, slot, (s, (p + step) * 2 + c)):
                 if begin:
                     copy.start()
                 else:
                     copy.wait_send()
 
+        @pl.when(at > p)
+        def _():
+            go(at, 1)
+
         @pl.when((at < p) & ((at != p - 1) | (at == 0)))
         def _():
-            for copy in maker(at)(at, (s, (p - 1) * 2 + c)):
-                if begin:
-                    copy.start()
-                else:
-                    copy.wait_send()
+            go(at, -1)
 
         @pl.when((at < p) & (at == p - 1) & (at > 0))
         def _():
-            for copy in maker(at)(nc, (s, (p - 1) * 2 + c)):
-                if begin:
-                    copy.start()
-                else:
-                    copy.wait_send()
-
-    def arrive(at, maker, slot):
-        for copy in maker(at)(slot, twin):
+            go(nc, -1)
+
+    def arrive(at, maker, half, slot):
+        for copy in maker(at, half, slot, twin):
             copy.wait_recv()
 
     def cases(at, body):
@@ -225,14 +234,20 @@
         def _():
             body(2)
 
+    def spread(d, half):
+        return remote(
+            own.at[p, c, half], gat.at[s, half], g_send.at[d, half], g_recv.at[d, half], across(d)
+        )
+
     def merge(at):
         for copy in twin_send(at):
             copy.wait_recv()
 
         def body(count):
+            places = (at, nc)[:count]
             sources = [(own.at[at, c], own_st.at[at, c]), (sib.at[at], sib_st.at[at])]
-            for slot in (at, nc)[:count]:
-                arrive(at, a_pair, slot)
+            for slot in places:
+                arrive(at, a_pair, 0, slot)
                 sources.append((chn.at[slot], chn_st.at[slot]))
             tops = [st[:heads] for _, st in sources]
             sums = [st[heads : 2 * heads] for _, st in sources]
@@ -244,21 +259,33 @@
             scales = [e * factor for e in scales]
             filler = jnp.zeros((128 - heads * len(scales), rows), F32)
             lanes = jnp.concatenate(scales + [filler], axis=0).T
-            for head in range(heads):
-                cut = slice(head * DH, (head + 1) * DH)
-                value = functools.reduce(
-                    jnp.add,
-                    [
-                        num[:, cut].astype(F32) * lanes[:, x * heads + head : x * heads + head + 1]
-                        for x, (num, _) in enumerate(sources)
-                    ],
-                )
-                own[at, c, :, cut] = value.astype(BF16)
             own_st[at, c, :heads] = top
             own_st[at, c, heads : 2 * heads] = total
+            for half in range(2):
+                if half == 1:
+                    for slot in places:
+                        arrive(at, a_pair, 1, slot)
+                for place in range(half_heads):
+                    cut = slice(place * DH, (place + 1) * DH)
+                    head = half * half_heads + place
+                    value = functools.reduce(
+                        jnp.add,
+                        [
+                            num[half, :, cut].astype(F32) * lanes[:, x * heads + head : x * heads + head + 1]
+                            for x, (num, _) in enumerate(sources)
+                        ],
+                    )
+                    own[at, c, half, :, cut] = value.astype(BF16)
+                if count < 2:
+                    move(at, a_pair, half, True)
+                if count > 0:
+                    @pl.when(done)
+                    def _():
+                        for d in range(1, ns):
+                            spread(d, half).start()
+                        gat[s, half] = own[p, c, half]
 
         cases(at, body)
-        move(at, a_pair, True)
 
     turns = nc + nc - nc // 2
 
@@ -288,44 +315,67 @@
         advance(i, merge)
         return carry
 
+    relay(turn(0))
     lax.fori_loop(0, turns, attention, 0)
 
-    def spread(d):
-        return remote(own.at[p, c], gat.at[s], g_send.at[d], g_recv.at[d], across(d))
-
-    for d in range(1, ns):
-        spread(d).start()
-    gat[s] = own[p, c]
     weight_copy.wait()
-    for d in range(1, ns):
-        spread(d).wait_recv()
+    for half in range(2):
+        for d in range(1, ns):
+            spread(d, half).wait_recv()
 
     def part_send(at):
         return remote(part.at[at, 1 - c], psib.at[at], bs_send.at[at], bs_recv.at[at], twin)
 
     def project(i):
         at = turn(i)
-        for side in range(2):
-            piece = gat[:, pl.ds(pl.multiple_of((at * 2 + side) * rows_here, rows_here), rows_here), :]
-            piece = piece.reshape(ns * rows_here, feats)
-            part[at, side] = jnp.dot(piece, wbuf[...], preferred_element_type=F32).astype(BF16)
+        mine = pl.ds(pl.multiple_of(at * 2 * rows_here, 2 * rows_here), 2 * rows_here)
+        pieces = [gat[:, half, mine, :].reshape(ns * 2 * rows_here, half_feats) for half in range(2)]
+        step = min(512, half_cols)
+        for lo in range(0, cols, step):
+            value = sum(
+                jnp.dot(
+                    piece, wbuf[half * half_feats : (half + 1) * half_feats, lo : lo + step],
+                    preferred_element_type=F32,
+                )
+                for half, piece in enumerate(pieces)
+            )
+            value = value.astype(BF16).reshape(ns, 2, rows_here, step)
+            half, at_col = lo // half_cols, lo % half_cols
+            for side in range(2):
+                part[at, side, half, :, at_col : at_col + step] = value[:, side].reshape(ns * rows_here, step)
         part_send(at).start()
+
+    def deliver(d, half):
+        to = (s + d) % ns
+        return remote(
+            part.at[p, c, half, span(to, rows_here), :], obuf.at[s, half],
+            o_send.at[d, half], o_recv.at[d, half], across(d),
+        )
 
     def add(at):
         part_send(at).wait_recv()
+        done = at == p
 
         def body(count):
-            sources = [part.at[at, c], psib.at[at]]
-            for slot in (at, nc)[:count]:
-                arrive(at, b_pair, slot)
-                sources.append(pchn.at[slot])
-            step = 512
-            for lo in range(0, cols, step):
-                value = functools.reduce(jnp.add, [x[:, lo : lo + step].astype(F32) for x in sources])
-                part[at, c, :, lo : lo + step] = value.astype(BF16)
+            places = (at, nc)[:count]
+            sources = [part.at[at, c], psib.at[at]] + [pchn.at[slot] for slot in places]
+            for half in range(2):
+                for slot in places:
+                    arrive(at, b_pair, half, slot)
+                step = min(512, half_cols)
+                for lo in range(0, half_cols, step):
+                    value = functools.reduce(jnp.add, [x[half, :, lo : lo + step].astype(F32) for x in sources])
+                    part[at, c, half, :, lo : lo + step] = value.astype(BF16)
+                if count < 2:
+                    move(at, b_pair, half, True)
+                if count > 0:
+                    @pl.when(done)
+                    def _():
+                        for d in range(1, ns):
+                            deliver(d, half).start()
+                        obuf[s, half] = part[p, c, half, span(s, rows_here), :]
 
         cases(at, body)
-        move(at, b_pair, True)
 
     def projection(i, carry):
         @pl.when(i < nc)
@@ -336,16 +386,6 @@
         return carry
 
     lax.fori_loop(0, turns, projection, 0)
-
-    def deliver(d):
-        to = (s + d) % ns
-        return remote(
-            part.at[p, c, span(to, rows_here), :], obuf.at[s], o_send.at[d], o_recv.at[d], across(d)
-        )
-
-    for d in range(1, ns):
-        deliver(d).start()
-    obuf[s] = part[p, c, span(s, rows_here), :]
 
     def drain(i, carry):
         for d in range(1, nc):
@@ -355,18 +395,23 @@
         for copy in twin_send(i):
             copy.wait_send()
         part_send(i).wait_send()
-        move(i, a_pair, False)
-        move(i, b_pair, False)
+        for half in range(2):
+            move(i, a_pair, half, False)
+            move(i, b_pair, half, False)
         return carry
 
     lax.fori_loop(0, nc, drain, 0)
-    for d in range(1, ns):
-        spread(d).wait_send()
-        deliver(d).wait_recv()
-    for t in range(ns):
-        out_ref[:, t * cols : (t + 1) * cols] = obuf[t]
-    for d in range(1, ns):
-        deliver(d).wait_send()
+    for half in range(2):
+        for d in range(1, ns):
+            spread(d, half).wait_send()
+            deliver(d, half).wait_recv()
+    for x in range(ns):
+        for half in range(2):
+            lo = x * cols + half * half_cols
+            out_ref[:, lo : lo + half_cols] = obuf[x, half]
+    for half in range(2):
+        for d in range(1, ns):
+            deliver(d, half).wait_send()
 
 
 def shards(n, ns, queries, probes, keys, values, w_out):
@@ -403,17 +448,17 @@
             vm((slots, local_keys, wide), BF16),
             vm((slots, local_keys, wide), BF16),
             vm((feats, cols), BF16),
-            vm((nc, 2, rows, feats), BF16),
+            vm((nc, 2, 2, rows, feats // 2), BF16),
             vm((nc, 2, st_rows, rows), F32),
-            vm((nc, rows, feats), BF16),
+            vm((nc, 2, rows, feats // 2), BF16),
             vm((nc, st_rows, rows), F32),
-            vm((nc + 1, rows, feats), BF16),
+            vm((nc + 1, 2, rows, feats // 2), BF16),
             vm((nc + 1, st_rows, rows), F32),
-            vm((ns, rows, feats), BF16),
-            vm((nc, 2, ns * rows_here, cols), BF16),
-            vm((nc, ns * rows_here, cols), BF16),
-            vm((nc + 1, ns * rows_here, cols), BF16),
-            vm((ns, rows_here, cols), BF16),
+            vm((ns, 2, rows, feats // 2), BF16),
+            vm((nc, 2, 2, ns * rows_here, cols // 2), BF16),
+            vm((nc, 2, ns * rows_here, cols // 2), BF16),
+            vm((nc + 1, 2, ns * rows_here, cols // 2), BF16),
+            vm((ns, 2, rows_here, cols // 2), BF16),
             dma((slots, 2)),
             dma((1,)),
             dma((nc,)),
@@ -423,16 +468,16 @@
             dma((nc, nc)),
             dma((nc, 2)),
             dma((nc, 2)),
+            dma((nc, 3)),
+            dma((nc + 1, 3)),
+            dma((ns, 2)),
+            dma((ns, 2)),
+            dma((nc,)),
+            dma((nc,)),
             dma((nc, 2)),
             dma((nc + 1, 2)),
-            dma((ns,)),
-            dma((ns,)),
-            dma((nc,)),
-            dma((nc,)),
-            dma((nc, 1)),
-            dma((nc + 1, 1)),
-            dma((ns,)),
-            dma((ns,)),
+            dma((ns, 2)),
+            dma((ns, 2)),
         ],
         compiler_params=pltpu.CompilerParams(
             collective_id=0, has_side_effects=True, vmem_limit_bytes=60 * 1024 * 1024

time: 111 us -> 96.3 us (0.87)
  Pallas kernels: 107 us -> 92.3 us
    pallas_call x1, Pallas kernels: 107 us -> 92.3 us  [shards(): pl.pallas_call(functools.partial(kernel, n, ns), out_shape=jax.ShapeDtype...]
where the time goes in v3:
time: 96.3 us; the launch traced here: 96.1 us
  Pallas kernels  92.3 us (96%)
  local copies, waits for them, and re-layouts  2.51 us (3%)
  other arithmetic  1.26 us (1%)
    pallas_call x1, Pallas kernels, shards(): pl.pallas_call(functools.partial(kernel, n, ns), out_shape=jax.ShapeDtype...  92.3 us

profile of v3, /device:TPU:0, one launch (start us, length us, event | category | flops | bytes accessed | tf_op | source)
XLA Modules:
  0.0 96.1 jit_solution(5036523188691059014)
XLA Ops:
  0.0 1.2 %compare_reduce_fusion = pred[128,64,2]{0,2,1:T(4,128)(4,1)S(1)} fusion(s32[128,64,8]{0,2,1:T(8,128)} %param.6, s32[2]{0:T(128)S(1)} %iota_add_fusion), kind=kLoop, calls=%fused_computation | loop fusion | flops 245760 | bytes 278536 | tf_op jit(solution)/shard_map/reduce_or | solution.py:429
  1.3 0.8 copy.9
  2.1 92.3 %shard_map.55 = bf16[16,8192]{1,0:T(8,128)(2,1)} custom-call(bf16[16,8192]{1,0:T(8,128)(2,1)} %q_ref.1, f32[4,128,32]{2,1,0:T(8,128)} %bitcast.2, bf16[1,512,8192]{2,1,0:T(8,128)(2,1)} %k_ref.1, bf16[1,512,8192]{2,1,0:T(8,128)(2,1)} %v_ref.1, bf16[1024,2048]{1,0:T(8,128)(2,1)} %w_ref.1), custom_call_target="tpu_custom_call" | custom-call | flops 4294967296 | bytes 20971520 | tf_op jit(solution)/shard_map/pallas_call | solution.py:435
  94.5 1.7 %copy.11 = bf16[16,8192]{1,0:T(8,128)(2,1)} copy(bf16[16,8192]{1,0:T(8,128)(2,1)} %shard_map.55) | data formatting | bytes 524288
  (2 shorter events, 0.1 us)

commit v4 on v3

--- a/solution.py
+++ b/solution.py
@@ -19,7 +19,7 @@
 
 def kernel(
     n, ns, q_ref, bias_ref, k_ref, v_ref, w_ref, out_ref,
-    qg, kbuf, vbuf, wbuf, own, own_st, sib, sib_st, chn, chn_st, gat, part, psib, pchn, obuf,
+    qg, kbuf, vbuf, wbuf, own, own_st, sib, sib_st, chn, chn_st, fin, gat, part, psib, pchn, obuf,
     kv_sem, w_sem, q_sem, qs_send, qs_recv, rl_send, rl_recv, as_send, as_recv, ac_send, ac_recv,
     g_send, g_recv, bs_send, bs_recv, bc_send, bc_recv, o_send, o_recv,
 ):
@@ -114,8 +114,6 @@
             copy.start()
     weight_copy.start()
 
-    lane = lax.broadcasted_iota(jnp.int32, (rows, 128), 1)
-
     def twin_send(at):
         return (
             remote(own.at[at, 1 - c], sib.at[at], as_send.at[at, 0], as_recv.at[at, 0], twin),
@@ -140,35 +138,35 @@
         def raw(x):
             cut = slice(x * DH, (x + 1) * DH)
             return lax.dot_general(
-                qg[at, :, cut], kbuf[slot, :, cut], (((1,), (1,)), ((), ())), preferred_element_type=F32
+                kbuf[slot, :, cut], qg[at, :, cut], (((1,), (1,)), ((), ())), preferred_element_type=F32
             )
 
         scores = raw(0)
         for side in range(2):
-            stats = jnp.zeros((rows, 128), F32)
             for head in range(heads):
                 x = side * heads + head
                 later = raw(x + 1) if x + 1 < 2 * heads else None
-                pieces = []
-                for b in range(blocks):
-                    lane_at = x * blocks + b
-                    pieces.append(
-                        scores[:, b * BLOCK : (b + 1) * BLOCK] + bias_ref[at, :, lane_at : lane_at + 1]
-                    )
+                pieces = [scores[b * BLOCK : (b + 1) * BLOCK] for b in range(blocks)]
+                biases = [bias_ref[at, x * blocks + b : x * blocks + b + 1, :] for b in range(blocks)]
                 top = functools.reduce(
-                    jnp.maximum, [jnp.max(piece, axis=1, keepdims=True) for piece in pieces]
+                    jnp.maximum,
+                    [jnp.max(piece, axis=0, keepdims=True) + bias for piece, bias in zip(pieces, biases)],
                 )
-                weights = jnp.concatenate([jnp.exp2((piece - top) * RATE) for piece in pieces], axis=1)
-                total = jnp.sum(weights, axis=1, keepdims=True)
-                numer = jnp.dot(
-                    weights.astype(BF16), vbuf[slot, :, x * DH : (x + 1) * DH], preferred_element_type=F32
+                shifts = [jnp.where(bias < 0.0, LOW, -top) for bias in biases]
+                weights = [jnp.exp2((piece + shift) * RATE) for piece, shift in zip(pieces, shifts)]
+                total = functools.reduce(jnp.add, [jnp.sum(w, axis=0, keepdims=True) for w in weights])
+                numer = lax.dot_general(
+                    vbuf[slot, :, x * DH : (x + 1) * DH],
+                    jnp.concatenate([w.astype(BF16) for w in weights], axis=0),
+                    (((0,), (0,)), ((), ())), preferred_element_type=F32,
                 )
                 half, place = head // half_heads, head % half_heads
-                own[at, side, half, :, place * DH : (place + 1) * DH] = numer.astype(BF16)
-                stats = jnp.where(lane == head, top, stats)
-                stats = jnp.where(lane == heads + head, total, stats)
+                own[at, side, half, place * DH : (place + 1) * DH, :] = numer.astype(BF16)
+                own_st[at, side, head : head + 1, :] = top
+                own_st[at, side, heads + head : heads + head + 1, :] = total
                 scores = later
-            own_st[at, side] = stats.T[:st_rows]
+            if 2 * heads < st_rows:
+                own_st[at, side, 2 * heads :, :] = jnp.zeros((st_rows - 2 * heads, rows), F32)
             if side == 0:
                 @pl.when(i + 1 < nc)
                 def _():
@@ -236,7 +234,7 @@
 
     def spread(d, half):
         return remote(
-            own.at[p, c, half], gat.at[s, half], g_send.at[d, half], g_recv.at[d, half], across(d)
+            fin.at[half], gat.at[s, half], g_send.at[d, half], g_recv.at[d, half], across(d)
         )
 
     def merge(at):
@@ -257,8 +255,6 @@
             done = at == p
             factor = jnp.where(done, 1.0 / total, jnp.ones_like(total))
             scales = [e * factor for e in scales]
-            filler = jnp.zeros((128 - heads * len(scales), rows), F32)
-            lanes = jnp.concatenate(scales + [filler], axis=0).T
             own_st[at, c, :heads] = top
             own_st[at, c, heads : 2 * heads] = total
             for half in range(2):
@@ -271,19 +267,22 @@
                     value = functools.reduce(
                         jnp.add,
                         [
-                            num[half, :, cut].astype(F32) * lanes[:, x * heads + head : x * heads + head + 1]
-                            for x, (num, _) in enumerate(sources)
+                            num[half, cut, :].astype(F32) * scale[head : head + 1]
+                            for scale, (num, _) in zip(scales, sources)
                         ],
                     )
-                    own[at, c, half, :, cut] = value.astype(BF16)
+                    own[at, c, half, cut, :] = value.astype(BF16)
                 if count < 2:
                     move(at, a_pair, half, True)
                 if count > 0:
                     @pl.when(done)
                     def _():
+                        for place in range(half_heads):
+                            cut = slice(place * DH, (place + 1) * DH)
+                            fin[half, :, cut] = own[p, c, half, cut, :].astype(F32).T.astype(BF16)
                         for d in range(1, ns):
                             spread(d, half).start()
-                        gat[s, half] = own[p, c, half]
+                        gat[s, half] = fin[half]
 
         cases(at, body)
 
@@ -427,8 +426,8 @@
     slots = min(nc, 4)
     block_ids = lax.axis_index("mem") * local_blocks + jnp.arange(local_blocks, dtype=jnp.int32)
     probed = jnp.any(probes[:, :, :, None] == block_ids[None, None, None, :], axis=2)
-    bias = jnp.where(probed, 0.0, LOW).astype(F32).reshape(rows, nc, 2 * heads * local_blocks)
-    bias = jnp.transpose(bias, (1, 0, 2))
+    bias = jnp.where(probed, 0.0, LOW).astype(F32)
+    bias = jnp.transpose(bias, (1, 2, 0)).reshape(nc, 2 * heads * local_blocks, rows)
     dma = pltpu.SemaphoreType.DMA
     vm = pltpu.VMEM
     flops = 4 * rows * width * local_keys + 2 * ns * rows * feats * cols
@@ -448,12 +447,13 @@
             vm((slots, local_keys, wide), BF16),
             vm((slots, local_keys, wide), BF16),
             vm((feats, cols), BF16),
-            vm((nc, 2, 2, rows, feats // 2), BF16),
+            vm((nc, 2, 2, feats // 2, rows), BF16),
             vm((nc, 2, st_rows, rows), F32),
-            vm((nc, 2, rows, feats // 2), BF16),
+            vm((nc, 2, feats // 2, rows), BF16),
             vm((nc, st_rows, rows), F32),
-            vm((nc + 1, 2, rows, feats // 2), BF16),
+            vm((nc + 1, 2, feats // 2, rows), BF16),
             vm((nc + 1, st_rows, rows), F32),
+            vm((2, rows, feats // 2), BF16),
             vm((ns, 2, rows, feats // 2), BF16),
             vm((nc, 2, 2, ns * rows_here, cols // 2), BF16),
             vm((nc, 2, ns * rows_here, cols // 2), BF16),

time: 96.3 us -> 92.8 us (0.964)
  Pallas kernels: 92.3 us -> 89 us
    pallas_call x1, Pallas kernels: 92.3 us -> 89 us  [shards(): pl.pallas_call(functools.partial(kernel, n, ns), out_shape=jax.ShapeDtype...]
where the time goes in v4:
time: 92.8 us; the launch traced here: 92.6 us
  Pallas kernels  89 us (96%)
  other arithmetic  1.89 us (2%)
  local copies, waits for them, and re-layouts  1.67 us (2%)
    pallas_call x1, Pallas kernels, shards(): pl.pallas_call(functools.partial(kernel, n, ns), out_shape=jax.ShapeDtype...  89 us

profile of v4, /device:TPU:0, one launch (start us, length us, event | category | flops | bytes accessed | tf_op | source)
XLA Modules:
  0.0 92.6 jit_solution(16705822131520625227)
XLA Ops:
  0.0 1.2 %compare_reduce_fusion = pred[128,64,2]{0,2,1:T(4,128)(4,1)S(1)} fusion(s32[128,64,8]{0,2,1:T(8,128)} %param.6, s32[2]{0:T(128)S(1)} %iota_add_fusion), kind=kLoop, calls=%fused_computation | loop fusion | flops 245760 | bytes 278536 | tf_op jit(solution)/shard_map/reduce_or | solution.py:428
  1.2 0.7 broadcast_select_fusion
  1.9 89.0 %shard_map.55 = bf16[16,8192]{1,0:T(8,128)(2,1)} custom-call(bf16[16,8192]{1,0:T(8,128)(2,1)} %q_ref.1, f32[4,32,128]{2,1,0:T(8,128)} %bitcast.3, bf16[1,512,8192]{2,1,0:T(8,128)(2,1)} %k_ref.1, bf16[1,512,8192]{2,1,0:T(8,128)(2,1)} %v_ref.1, bf16[1024,2048]{1,0:T(8,128)(2,1)} %w_ref.1), custom_call_target="tpu_custom_call" | custom-call | flops 4294967296 | bytes 20971520 | tf_op jit(solution)/shard_map/pallas_call | solution.py:434
  90.9 1.7 %copy.8 = bf16[16,8192]{1,0:T(8,128)(2,1)} copy(bf16[16,8192]{1,0:T(8,128)(2,1)} %shard_map.55) | data formatting | bytes 524288
  (1 shorter events, 0.0 us)

commit v5 on v4

--- a/solution.py
+++ b/solution.py
@@ -35,7 +35,7 @@
     keys = kbuf.shape[1]
     blocks = keys // BLOCK
     cols = wbuf.shape[1]
-    half_cols = cols // 2
+    fold = ns // 2
     st_rows = own_st.shape[2]
     s = lax.axis_index("seq")
     me = lax.axis_index("mem")
@@ -47,7 +47,10 @@
         return (s, ((p + d) % nc) * 2 + c)
 
     def across(d):
-        return ((s + d) % ns, me)
+        return (((s // 2 + d // 2) % fold) * 2 + (s % 2 + d % 2) % 2, me)
+
+    def origin(d):
+        return (((s // 2 + fold - d // 2) % fold) * 2 + (s % 2 + d % 2) % 2, me)
 
     def turn(i):
         return (i % 2) * (nc - 1 - i // 2) + (1 - i % 2) * (i // 2)
@@ -234,7 +237,7 @@
 
     def spread(d, half):
         return remote(
-            fin.at[half], gat.at[s, half], g_send.at[d, half], g_recv.at[d, half], across(d)
+            fin.at[half], gat.at[d, half], g_send.at[d, half], g_recv.at[d, half], across(d)
         )
 
     def merge(at):
@@ -282,16 +285,13 @@
                             fin[half, :, cut] = own[p, c, half, cut, :].astype(F32).T.astype(BF16)
                         for d in range(1, ns):
                             spread(d, half).start()
-                        gat[s, half] = fin[half]
+                        gat[0, half] = fin[half]
 
         cases(at, body)
 
     turns = nc + nc - nc // 2
 
-    def advance(i, join):
-        late = i // nc
-        k = (1 - late) * (i // 2) + late * (i - nc + nc // 2)
-
+    def stream(k, join):
         def one(side, carry):
             dest = (1 - side) * (nc - 1 - k + p) + side * (k - nc + 1 + p)
             wanted = ((side == 0) & (dest < nc)) | ((side == 1) & (dest >= 0) & (dest < p))
@@ -302,9 +302,14 @@
 
             return carry
 
+        lax.fori_loop(0, 2, one, 0)
+
+    def advance(i, join):
+        late = i // nc
+
         @pl.when((late == 1) | (i % 2 == 1))
         def _():
-            lax.fori_loop(0, 2, one, 0)
+            stream((1 - late) * (i // 2) + late * (i - nc + nc // 2), join)
 
     def attention(i, carry):
         @pl.when(i < nc)
@@ -317,52 +322,59 @@
     relay(turn(0))
     lax.fori_loop(0, turns, attention, 0)
 
-    weight_copy.wait()
-    for half in range(2):
-        for d in range(1, ns):
-            spread(d, half).wait_recv()
-
-    def part_send(at):
-        return remote(part.at[at, 1 - c], psib.at[at], bs_send.at[at], bs_recv.at[at], twin)
-
-    def project(i):
-        at = turn(i)
-        mine = pl.ds(pl.multiple_of(at * 2 * rows_here, 2 * rows_here), 2 * rows_here)
-        pieces = [gat[:, half, mine, :].reshape(ns * 2 * rows_here, half_feats) for half in range(2)]
-        step = min(512, half_cols)
-        for lo in range(0, cols, step):
-            value = sum(
-                jnp.dot(
-                    piece, wbuf[half * half_feats : (half + 1) * half_feats, lo : lo + step],
-                    preferred_element_type=F32,
+    def part_send(at, half):
+        return remote(
+            part.at[at, 1 - c, half], psib.at[at, half], bs_send.at[at, half], bs_recv.at[at, half], twin
+        )
+
+    def project(half):
+        for d in range(max(1, half * fold), (half + 1) * fold):
+            for x in range(2):
+                spread(d, x).wait_recv()
+
+        def one(i, carry):
+            at = turn(i)
+            mine = pl.ds(pl.multiple_of(at * 2 * rows_here, 2 * rows_here), 2 * rows_here)
+            pieces = [
+                gat[half * fold : (half + 1) * fold, x, mine, :].reshape(fold * 2 * rows_here, half_feats)
+                for x in range(2)
+            ]
+            step = min(512, cols)
+            for lo in range(0, cols, step):
+                value = sum(
+                    jnp.dot(
+                        piece, wbuf[x * half_feats : (x + 1) * half_feats, lo : lo + step],
+                        preferred_element_type=F32,
+                    )
+                    for x, piece in enumerate(pieces)
                 )
-                for half, piece in enumerate(pieces)
-            )
-            value = value.astype(BF16).reshape(ns, 2, rows_here, step)
-            half, at_col = lo // half_cols, lo % half_cols
-            for side in range(2):
-                part[at, side, half, :, at_col : at_col + step] = value[:, side].reshape(ns * rows_here, step)
-        part_send(at).start()
-
-    def deliver(d, half):
-        to = (s + d) % ns
+                value = value.astype(BF16).reshape(fold, 2, rows_here, step)
+                for side in range(2):
+                    part[at, side, half, :, lo : lo + step] = value[:, side].reshape(fold * rows_here, step)
+            part_send(at, half).start()
+            return carry
+
+        lax.fori_loop(0, nc, one, 0)
+
+    def deliver(d):
+        half, place = d // fold, d % fold
         return remote(
-            part.at[p, c, half, span(to, rows_here), :], obuf.at[s, half],
-            o_send.at[d, half], o_recv.at[d, half], across(d),
-        )
-
-    def add(at):
-        part_send(at).wait_recv()
-        done = at == p
-
-        def body(count):
-            places = (at, nc)[:count]
-            sources = [part.at[at, c], psib.at[at]] + [pchn.at[slot] for slot in places]
-            for half in range(2):
+            part.at[p, c, half, place * rows_here : (place + 1) * rows_here, :], obuf.at[s],
+            o_send.at[d], o_recv.at[d], origin(d),
+        )
+
+    def add(half):
+        def join(at):
+            part_send(at, half).wait_recv()
+            done = at == p
+
+            def body(count):
+                places = (at, nc)[:count]
+                sources = [part.at[at, c], psib.at[at]] + [pchn.at[slot] for slot in places]
                 for slot in places:
                     arrive(at, b_pair, half, slot)
-                step = min(512, half_cols)
-                for lo in range(0, half_cols, step):
+                step = min(512, cols)
+                for lo in range(0, cols, step):
                     value = functools.reduce(jnp.add, [x[half, :, lo : lo + step].astype(F32) for x in sources])
                     part[at, c, half, :, lo : lo + step] = value.astype(BF16)
                 if count < 2:
@@ -370,21 +382,27 @@
                 if count > 0:
                     @pl.when(done)
                     def _():
-                        for d in range(1, ns):
-                            deliver(d, half).start()
-                        obuf[s, half] = part[p, c, half, span(s, rows_here), :]
-
-        cases(at, body)
-
-    def projection(i, carry):
-        @pl.when(i < nc)
-        def _():
-            project(i)
-
-        advance(i, add)
+                        for d in range(max(1, half * fold), (half + 1) * fold):
+                            deliver(d).start()
+                        if half == 0:
+                            obuf[s] = part[p, c, 0, :rows_here, :]
+
+            cases(at, body)
+
+        return join
+
+    weight_copy.wait()
+    project(0)
+    stream(0, add(0))
+    project(1)
+    stream(0, add(1))
+
+    def summing(k, carry):
+        stream(k, add(0))
+        stream(k, add(1))
         return carry
 
-    lax.fori_loop(0, turns, projection, 0)
+    lax.fori_loop(1, nc, summing, 0)
 
     def drain(i, carry):
         for d in range(1, nc):
@@ -393,24 +411,22 @@
         query_twin(i).wait_send()
         for copy in twin_send(i):
             copy.wait_send()
-        part_send(i).wait_send()
+        for half in range(2):
+            part_send(i, half).wait_send()
         for half in range(2):
             move(i, a_pair, half, False)
             move(i, b_pair, half, False)
         return carry
 
     lax.fori_loop(0, nc, drain, 0)
-    for half in range(2):
-        for d in range(1, ns):
+    for d in range(1, ns):
+        for half in range(2):
             spread(d, half).wait_send()
-            deliver(d, half).wait_recv()
+        deliver(d).wait_recv()
     for x in range(ns):
-        for half in range(2):
-            lo = x * cols + half * half_cols
-            out_ref[:, lo : lo + half_cols] = obuf[x, half]
-    for half in range(2):
-        for d in range(1, ns):
-            deliver(d, half).wait_send()
+        out_ref[:, x * cols : (x + 1) * cols] = obuf[x]
+    for d in range(1, ns):
+        deliver(d).wait_send()
 
 
 def shards(n, ns, queries, probes, keys, values, w_out):
@@ -455,10 +471,10 @@
             vm((nc + 1, st_rows, rows), F32),
             vm((2, rows, feats // 2), BF16),
             vm((ns, 2, rows, feats // 2), BF16),
-            vm((nc, 2, 2, ns * rows_here, cols // 2), BF16),
-            vm((nc, 2, ns * rows_here, cols // 2), BF16),
-            vm((nc + 1, 2, ns * rows_here, cols // 2), BF16),
-            vm((ns, 2, rows_here, cols // 2), BF16),
+            vm((nc, 2, 2, ns // 2 * rows_here, cols), BF16),
+            vm((nc, 2, ns // 2 * rows_here, cols), BF16),
+            vm((nc + 1, 2, ns // 2 * rows_here, cols), BF16),
+            vm((ns, rows_here, cols), BF16),
             dma((slots, 2)),
             dma((1,)),
             dma((nc,)),
@@ -472,12 +488,12 @@
             dma((nc + 1, 3)),
             dma((ns, 2)),
             dma((ns, 2)),
-            dma((nc,)),
-            dma((nc,)),
+            dma((nc, 2)),
+            dma((nc, 2)),
             dma((nc, 2)),
             dma((nc + 1, 2)),
-            dma((ns, 2)),
-            dma((ns, 2)),
+            dma((ns,)),
+            dma((ns,)),
         ],
         compiler_params=pltpu.CompilerParams(
             collective_id=0, has_side_effects=True, vmem_limit_bytes=60 * 1024 * 1024

time: 92.8 us -> 91 us (0.981)
  Pallas kernels: 89 us -> 87.2 us
    pallas_call x1, Pallas kernels: 89 us -> 87.2 us  [shards(): pl.pallas_call(functools.partial(kernel, n, ns), out_shape=jax.ShapeDtype...]
where the time goes in v5:
time: 91 us; the launch traced here: 90.8 us
  Pallas kernels  87.2 us (96%)
  other arithmetic  1.89 us (2%)
  local copies, waits for them, and re-layouts  1.67 us (2%)
    pallas_call x1, Pallas kernels, shards(): pl.pallas_call(functools.partial(kernel, n, ns), out_shape=jax.ShapeDtype...  87.2 us

profile of v5, /device:TPU:0, one launch (start us, length us, event | category | flops | bytes accessed | tf_op | source)
XLA Modules:
  0.0 90.8 jit_solution(17622119648930200653)
XLA Ops:
  0.0 1.2 %compare_reduce_fusion = pred[128,64,2]{0,2,1:T(4,128)(4,1)S(1)} fusion(s32[128,64,8]{0,2,1:T(8,128)} %param.6, s32[2]{0:T(128)S(1)} %iota_add_fusion), kind=kLoop, calls=%fused_computation | loop fusion | flops 245760 | bytes 278536 | tf_op jit(solution)/shard_map/reduce_or | solution.py:444
  1.2 0.7 broadcast_select_fusion
  1.9 87.2 %shard_map.55 = bf16[16,8192]{1,0:T(8,128)(2,1)} custom-call(bf16[16,8192]{1,0:T(8,128)(2,1)} %q_ref.1, f32[4,32,128]{2,1,0:T(8,128)} %bitcast.3, bf16[1,512,8192]{2,1,0:T(8,128)(2,1)} %k_ref.1, bf16[1,512,8192]{2,1,0:T(8,128)(2,1)} %v_ref.1, bf16[1024,2048]{1,0:T(8,128)(2,1)} %w_ref.1), custom_call_target="tpu_custom_call" | custom-call | flops 4294967296 | bytes 20971520 | tf_op jit(solution)/shard_map/pallas_call | solution.py:450
  89.1 1.7 %copy.8 = bf16[16,8192]{1,0:T(8,128)(2,1)} copy(bf16[16,8192]{1,0:T(8,128)(2,1)} %shard_map.55) | data formatting | bytes 524288
  (1 shorter events, 0.0 us)
